TPU v7x, 128 devices: a whole 4x4x4 slice. The times are simulated.
128 devices in a mesh: dp: 16 (over x_hi, y, core), tensor: 8 (over z, x_lo).
Axes of the slice: x: 4 (x_hi: 2, x_lo: 2; x = x_hi * 2 + x_lo), y: 4, z: 4, core: 2. Of those that a mesh axis runs over, the one named last changes fastest.
Arguments:
- hidden: bfloat16 [2, 16, 512, 1536], P(None, 'dp', 'tensor'), may hold values from -6 to 6
- condition: bfloat16 [2, 16, 1024], P(None, 'dp'), may hold values from -6 to 6
- caption: bfloat16 [2, 16, 256, 4096], P(None, 'dp'), may hold values from -6 to 6
- lengths: int32 [2, 16], P(None, 'dp'), may hold values from 128 to 512, as said below
- frames: int32 [2, 16], P(None, 'dp'), may hold values from 1 to 4
- widths: int32 [2, 16], P(None, 'dp'), may hold values from 8 to 32
- caption_lens: int32 [2, 16], P(None, 'dp'), may hold values from 32 to 256, as said below
- cotangent: bfloat16 [2, 16, 512, 1536], P(None, 'dp', 'tensor'), may hold values from -6 to 6
- ada_weight: bfloat16 [1024, 6144], P('dp', 'tensor'), may hold values from -0.1875 to 0.1875
- ada_bias: bfloat16 [6144], P('dp'), may hold values from -3 to 3
- norm_gains: bfloat16 [4, 1536], P(None, 'dp'), may hold values from 0.25 to 1.75
- qkv_weight: bfloat16 [3, 1536, 1536], P(None, 'dp', 'tensor'), may hold values from -0.15625 to 0.15625
- head_gains: bfloat16 [3, 64], replicated, may hold values from 0.25 to 1.75
- caption_weight: bfloat16 [2, 4096, 1536], P(None, 'dp', 'tensor'), may hold values from -0.09375 to 0.09375
- head_gate: bfloat16 [24], replicated, may hold values from -1.5 to 1.5
- out_weight: bfloat16 [1536, 1536], P('tensor', 'dp'), may hold values from -0.15625 to 0.15625
- ffn_weight: bfloat16 [2, 1536, 4096], P(None, 'dp', 'tensor'), may hold values from -0.15625 to 0.15625
- down_weight: bfloat16 [4096, 1536], P('tensor', 'dp'), may hold values from -0.09375 to 0.09375
Outputs:
- layer_out: bfloat16 [2, 16, 512, 1536], P(None, 'dp', 'tensor')
- grad_hidden: float32 [2, 16, 512, 1536], P(None, 'dp', 'tensor')
- grad_ada_weight: float32 [1024, 6144], P('dp', 'tensor')
- grad_ada_bias: float32 [6144], P('dp')
- grad_norm_gains: float32 [4, 1536], P(None, 'dp')
- grad_qkv_weight: float32 [3, 1536, 1536], P(None, 'dp', 'tensor')
- grad_head_gains: float32 [3, 64], replicated
- grad_caption_weight: float32 [2, 4096, 1536], P(None, 'dp', 'tensor')
- grad_head_gate: float32 [24], replicated
- grad_out_weight: float32 [1536, 1536], P('tensor', 'dp')
- grad_ffn_weight: float32 [2, 1536, 4096], P(None, 'dp', 'tensor')
- grad_down_weight: float32 [4096, 1536], P('tensor', 'dp')
Inputs may be any that keep to these rules, and one draw needn't show every extreme that they name: `lengths`: for every item index, one of the 2 micro-batches holds an item with all 512 slots live. `caption_lens`: for every item index, one of the 2 micro-batches holds an item with all 256 caption slots live.
All inputs are finite; a program needn't handle non-finite values.
Results may differ from a plain program's by a relative error of at most 0.023.
Values may be sent and summed in bfloat16 or wider, within the bound.
A program may use at most 192 MiB of HBM per device.

v0:
```python
import jax
import jax.numpy as jnp
from jax import lax
from jax.experimental import pallas as pl
from jax.experimental.pallas import tpu as pltpu
from jax.sharding import PartitionSpec as P

D = 1536
H = 24
HD = 64
EPSILON = 1e-05
NEGATIVE = -1e30
MESH = pl.DeviceIdType.MESH
VMEM = pltpu.VMEM
F32 = jnp.float32
BF16 = jnp.bfloat16


def coords():
    dp = lax.axis_index("dp")
    t = lax.axis_index("tensor")
    return dp // 8, t % 2, (dp // 2) % 4, t // 2, dp % 2


def device_of(x, y, z, c):
    return ((x // 2) * 8 + y * 2 + c, z * 2 + x % 2)


def greet_signal(devices):
    barrier = pltpu.get_barrier_semaphore()
    for device in devices:
        pl.semaphore_signal(barrier, inc=1, device_id=device, device_id_type=MESH)


def greet_wait(devices):
    pl.semaphore_wait(pltpu.get_barrier_semaphore(), len(devices))


def greet(devices):
    greet_signal(devices)
    greet_wait(devices)


class Sender:
    def __init__(self, send_sem, recv_sem):
        self.send_sem = send_sem
        self.recv_sem = recv_sem
        self.copies = []

    def __call__(self, src, dst, device):
        k = len(self.copies)
        copy = pltpu.make_async_remote_copy(
            src_ref=src,
            dst_ref=dst,
            send_sem=self.send_sem.at[k],
            recv_sem=self.recv_sem.at[k],
            device_id=device,
            device_id_type=MESH,
        )
        copy.start()
        self.copies.append(copy)
        return copy

    def drain(self):
        for copy in self.copies:
            copy.wait_send()


def dma_sems(n):
    return [pltpu.SemaphoreType.DMA((n,)), pltpu.SemaphoreType.DMA((n,))]


def plane_peers():
    xh, xl, y, z, c = coords()
    x = 2 * xh + xl
    xr, xq = (x + 1) % 4, (x + 3) % 4
    yr, yq = (y + 1) % 4, (y + 3) % 4
    peers = [
        device_of(xr, y, z, c),
        device_of(xq, y, z, c),
        device_of(x, yr, z, c),
        device_of(x, yq, z, c),
        device_of(x, y, z, 1 - c),
        device_of((x + 2) % 4, y, z, c),
        device_of(x, (y + 2) % 4, z, c),
    ]
    return x, y, c, xr, xq, yr, yq, peers


def add_low(a, b):
    return (a.astype(F32) + b.astype(F32)).astype(BF16)


def normalize(values):
    inverse = lax.rsqrt(jnp.mean(values * values, axis=-1, keepdims=True) + EPSILON)
    return (values * inverse, inverse)


def norm_back(unit_values, inverse, gradient):
    return inverse * (
        gradient - unit_values * jnp.mean(gradient * unit_values, axis=-1, keepdims=True)
    )


def swish(values):
    return values * jax.nn.sigmoid(values)


def z_ring():
    xh, xl, y, z, c = coords()
    x = 2 * xh + xl
    return z, device_of(x, y, (z + 1) % 4, c), device_of(x, y, (z + 3) % 4, c)


class ZGather:
    def __init__(self, send, own, every, right, left):
        self.send, self.every, self.right, self.left = send, every, right, left
        half = every.shape[1] // 2
        self.lower, self.upper = pl.ds(0, half), pl.ds(half, half)
        self.a_low = send(own.at[self.lower], every.at[1, self.lower], right)
        self.b_up = send(own.at[self.upper], every.at[2, self.upper], left)
        self.a_up = send(own.at[self.upper], every.at[1, self.upper], right)
        self.b_low = send(own.at[self.lower], every.at[2, self.lower], left)

    def near(self):
        every, lower, upper = self.every, self.lower, self.upper
        self.a_low.wait_recv()
        self.far_low = self.send(every.at[1, lower], every.at[3, lower], self.right)
        self.b_up.wait_recv()
        self.far_up = self.send(every.at[2, upper], every.at[3, upper], self.left)
        self.a_up.wait_recv()
        self.b_low.wait_recv()

    def far(self):
        self.far_low.wait_recv()
        self.far_up.wait_recv()


class ZScatter:
    def __init__(self, send, part, relay, got, right, left):
        self.send, self.part, self.relay, self.got = send, part, relay, got
        self.right, self.left = right, left
        self.lower, self.upper = pl.ds(0, 64), pl.ds(64, 64)
        self.waits = []

    def near(self):
        part, got = self.part, self.got
        self.waits.append(self.send(part.at[2, self.upper], got.at[0, self.upper], self.right))
        self.waits.append(self.send(part.at[1, self.lower], got.at[1, self.lower], self.left))

    def far(self):
        part, relay = self.part, self.relay
        self.relays = []
        for i in range(2):
            rows, low, up = pl.ds(32 * i, 32), pl.ds(32 * i, 32), pl.ds(64 + 32 * i, 32)
            self.relays.append(
                (
                    self.send(part.at[3, low], relay.at[0, rows], self.right),
                    self.send(part.at[3, up], relay.at[1, rows], self.left),
                )
            )

    def pass_on(self):
        part, relay, got = self.part, self.relay, self.got
        for i in range(2):
            rows, low, up = pl.ds(32 * i, 32), pl.ds(32 * i, 32), pl.ds(64 + 32 * i, 32)
            self.relays[i][0].wait_recv()
            part[2, low] = add_low(part[2, low], relay[0, rows])
            self.waits.append(self.send(part.at[2, low], got.at[0, low], self.right))
            self.relays[i][1].wait_recv()
            part[1, up] = add_low(part[1, up], relay[1, rows])
            self.waits.append(self.send(part.at[1, up], got.at[1, up], self.left))

    def total(self):
        for copy in self.waits:
            copy.wait_recv()
        got = self.got
        return self.part[0].astype(F32) + got[0].astype(F32) + got[1].astype(F32)


def mm(a, b):
    return lax.dot_general(a, b, (((1,), (0,)), ((), ())), preferred_element_type=F32)


def mm_t(a, b):
    return lax.dot_general(a, b, (((1,), (1,)), ((), ())), preferred_element_type=F32)


def tile(j, size=256):
    return pl.ds(pl.multiple_of(j * size, size), size)


def transpose_into(src, dst):
    def column(j, carry):
        cols = tile(j, 128)
        for slot in range(4):
            dst[cols, slot * 128 : (slot + 1) * 128] = src[slot, :, cols].T
        return carry

    lax.fori_loop(0, D // 128, column, 0)


class PlaneGather:
    def __init__(self, send, shard, every):
        self.send, self.shard, self.every = send, shard, every
        rows, cols = shard.shape
        half = rows // 2
        self.top, self.low = pl.ds(0, half), pl.ds(half, half)
        self.late = []

    def at(self, xx, yy, *rest):
        return self.every.at[(xx % 2, xx // 2, yy, self.c) + rest]

    def same(self, ref, device):
        return self.send(ref, ref, device)

    def to_sibling(self, ref):
        self.late.append(self.send(ref, ref, self.sibling))

    def start(self, local_sem):
        x, y, c, xr, xq, yr, yq, peers = plane_peers()
        self.x, self.y, self.c = x, y, c
        self.xr, self.xq, self.yr, self.yq = xr, xq, yr, yq
        self.go_xr, self.go_xq, self.go_yr, self.go_yq, self.sibling, go_xo, go_yo = peers
        shard, top, low = self.shard, self.top, self.low
        self.a_r = self.send(shard.at[top], self.at(x, y, top), self.go_xr)
        self.a_l = self.send(shard.at[top], self.at(x, y, top), self.go_xq)
        self.b_r = self.send(shard.at[low], self.at(x, y, low), self.go_yr)
        self.b_l = self.send(shard.at[low], self.at(x, y, low), self.go_yq)
        self.a_o = self.send(shard.at[top], self.at(x, y, top), go_xo)
        self.b_o = self.send(shard.at[low], self.at(x, y, low), go_yo)
        self.late.append(self.send(shard, self.at(x, y), self.sibling))
        self.local = pltpu.make_async_copy(shard, self.at(x, y), local_sem)
        self.local.start()

    def step3(self):
        x, y, c = self.x, self.y, self.c
        every, top, low = self.every, self.top, self.low
        self.local.wait()
        for copy in (self.a_r, self.a_l, self.a_o):
            copy.wait_recv()
        block = every.at[:, :, y, c, top]
        self.g_r = self.same(block, self.go_yr)
        self.g_l = self.same(block, self.go_yq)
        for copy in (self.b_r, self.b_l, self.b_o):
            copy.wait_recv()
        block = every.at[x % 2, x // 2, :, c, low]
        self.h_r = self.same(block, self.go_xr)
        self.h_l = self.same(block, self.go_xq)
        for k in range(1, 4):
            self.to_sibling(self.at((x + k) % 4, y, top))
            self.to_sibling(self.at(x, (y + k) % 4, low))

    def step4(self):
        c, every, top, low = self.c, self.every, self.top, self.low
        xr, xq, yr, yq = self.xr, self.xq, self.yr, self.yq
        self.g_r.wait_recv()
        self.f1 = self.same(every.at[0, :, yq, c, top], self.go_yr)
        self.g_l.wait_recv()
        self.f2 = self.same(every.at[1, :, yr, c, top], self.go_yq)
        self.h_r.wait_recv()
        self.f3 = self.same(every.at[xq % 2, xq // 2, pl.ds(0, 2), c, low], self.go_xr)
        self.h_l.wait_recv()
        self.f4 = self.same(every.at[xr % 2, xr // 2, pl.ds(2, 2), c, low], self.go_xq)
        self.to_sibling(every.at[:, :, yq, c, top])
        self.to_sibling(every.at[:, :, yr, c, top])
        self.to_sibling(every.at[xq % 2, xq // 2, :, c, low])
        self.to_sibling(every.at[xr % 2, xr // 2, :, c, low])

    def step5(self):
        c, every, top, low = self.c, self.every, self.top, self.low
        xo, yo = (self.x + 2) % 4, (self.y + 2) % 4
        for copy in (self.f1, self.f2, self.f3, self.f4):
            copy.wait_recv()
        self.to_sibling(every.at[:, :, yo, c, top])
        self.to_sibling(every.at[xo % 2, xo // 2, :, c, low])

    def finish(self):
        for copy in self.late:
            copy.wait_recv()


OFFSETS = (0, 3, 1, 2)


def lanes(shape):
    return lax.broadcasted_iota(jnp.int32, shape, len(shape) - 1)


def head_block():
    row = lax.broadcasted_iota(jnp.int32, (128, 128), 0) // 64
    col = lax.broadcasted_iota(jnp.int32, (128, 128), 1) // 64
    return jnp.where(row == col, 1.0 / 64.0, 0.0).astype(BF16)


def head_mean(values, block):
    high = values.astype(BF16)
    low = (values - high.astype(F32)).astype(BF16)
    return mm(high, block) + mm(low, block)


def swap_quarters(values):
    second = (lanes(values.shape) % 64) >= 32
    return jnp.where(second, pltpu.roll(values, 32, 1), pltpu.roll(values, 96, 1))


GAIN_ROW, GATE_ROW, LENGTH_ROW, FRAMES_ROW, WIDTH_ROW, TEXT_ROW, BIAS_ROW = 0, 3, 6, 7, 8, 9, 10


def key_bias(total, z, length):
    lane = lanes((1, total))
    if total == 512:
        slot = lane // 128
        block = jnp.where(slot == 0, z, jnp.where(slot == 1, z + 3, jnp.where(slot == 2, z + 1, z + 2)))
        position = (block % 4) * 128 + lane % 128
    else:
        position = lane
    return jnp.where(position.astype(F32) < length[:, :1], 0.0, NEGATIVE)


def fill_rope(cos_ref, sin_ref, z, length, frames, width):
    lane = lanes((128, 128))
    pair = lane % 32
    offset = jnp.where(pair >= 20, 20, jnp.where(pair >= 8, 8, 0))
    size = jnp.where(pair >= 8, 12.0, 8.0)
    freq = jnp.exp((pair - offset).astype(F32) / size * (-9.210340371976184))
    sign = jnp.where(lane % 64 >= 32, 1.0, -1.0)
    row_size = width
    per_frame = jnp.floor((length + frames - 0.5) / frames)
    row = lax.broadcasted_iota(jnp.int32, (128, 128), 0).astype(F32)
    for slot in range(4):
        start = (((z + OFFSETS[slot]) % 4) * 128).astype(F32)
        position = row + start
        frame = jnp.floor((position + 0.5) / per_frame)
        within = position - frame * per_frame
        row_pos = jnp.floor((within + 0.5) / row_size)
        col_pos = within - row_pos * row_size
        chosen = jnp.where(pair >= 20, col_pos, jnp.where(pair >= 8, row_pos, frame))
        angle = chosen * freq
        cos_ref[slot] = jnp.cos(angle)
        sin_ref[slot] = jnp.sin(angle) * sign


def attention_kernel(
    hid_ref,
    cot_ref,
    cap_hbm,
    cond_ref,
    gain_in,
    ada_ref,
    qkv_ref,
    out_w_ref,
    ffn_w_ref,
    down_t_ref,
    cap_t_ref,
    bias_ref,
    head_gain_ref,
    head_gate_ref,
    len_ref,
    frame_ref,
    width_ref,
    tlen_ref,
    w_f,
    w_a_out,
    cap_flip_out,
    first_flip_out,
    q8_out,
    kk_out,
    vv_out,
    qr_out,
    kr_out,
    tkr_out,
    other_out,
    lse_out,
    cw_out,
    cos_out,
    sin_out,
    resid_out,
    tk_out,
    tv_out,
    attn_out,
    mid_out,
    second_out,
    cot_out,
    mod_ref,
    gains_ref,
    got1,
    live_ref,
    facts,
    w_a,
    cap_flip,
    first_flip,
    q8,
    kk,
    vv,
    qr,
    kr,
    tkr,
    other_ref,
    lse_ref,
    cw,
    cos_ref,
    sin_ref,
    resid_ref,
    tk,
    tv,
    attn_ref,
    mid_ref,
    second_ref,
    first,
    own_ref,
    sh_a,
    sh_f,
    sh_c,
    w_c,
    cap,
    hid_all,
    hid_own,
    msg,
    sent2,
    got2,
    got3,
    mixed,
    part,
    relay,
    got,
    local_sems,
    ss,
    rs,
):
    dp = lax.axis_index("dp")
    t = lax.axis_index("tensor")
    xh, xl, y, z, c = coords()
    _, right, left = z_ring()
    pair = device_of(2 * xh + 1 - xl, y, z, c)
    dp_peers = [((dp + k) % 16, t) for k in range(1, 16)]
    t_peers = [(dp, (t + k) % 8) for k in range(1, 8)]
    outer_x = device_of((2 * xh + xl + 3 - 2 * xl) % 4, y, z, c)
    everyone = dp_peers + t_peers + [outer_x]
    greet_signal(everyone)
    load_cap = pltpu.make_async_copy(cap_hbm.at[xl], cap, local_sems.at[0])
    load_cap.start()
    load_hid = pltpu.make_async_copy(hid_ref.at[xl], hid_own.at[xl], local_sems.at[4])
    load_hid.start()
    flushes = []

    def flush(src, dst):
        copy = pltpu.make_async_copy(src, dst, local_sems.at[5 + len(flushes)])
        copy.start()
        flushes.append(copy)

    flush(cot_ref.at[xl], cot_out.at[xl])
    facts[...] = jnp.zeros((16, 128), F32)
    for i in range(3):
        gain = head_gain_ref[i : i + 1, :].astype(F32)
        facts[i : i + 1, 0:64] = gain
        facts[i : i + 1, 64:128] = gain
        facts[BIAS_ROW + i : BIAS_ROW + i + 1, :] = bias_ref[:, i * 128 : i * 128 + 128].astype(F32)
    gates = jnp.tanh(head_gate_ref[...].astype(F32))
    gate_lane = lanes((1, 24))
    low_row = lanes((1, 128)) < 64
    for p in range(3):
        a, b = [
            jnp.sum(jnp.where(gate_lane == z * 6 + h, gates, 0.0), axis=1, keepdims=True)
            for h in ((0, 1), (3, 4), (2, 5))[p]
        ]
        facts[GATE_ROW + p : GATE_ROW + p + 1, :] = jnp.where(low_row, a, b)
    for i, ref in enumerate((len_ref, frame_ref, width_ref, tlen_ref)):
        count = jnp.where(xl == 0, ref[:, 0:1], ref[:, 1:2]).astype(F32)
        facts[LENGTH_ROW + i : LENGTH_ROW + i + 1, :] = jnp.broadcast_to(count, (1, 128))
    unit = swish(cond_ref[...].astype(F32)).astype(BF16).astype(F32)
    msg[...] = jnp.zeros((16, 8, 128), F32)
    gain_rows = gain_in[...].astype(F32)
    for d in range(16):
        msg[d, 0:2, 0:64] = unit[:, d * 64 : (d + 1) * 64]
        msg[d, 4:8, 0:96] = gain_rows
    qs, ks, vs = qkv_ref[0], qkv_ref[1], qkv_ref[2]
    os = out_w_ref[...].T
    sh_a[...] = jnp.concatenate(
        [qs, ks[:, 128:192], ks[:, 0:128], vs, os[:, 128:192], os[:, 0:128]],
        axis=1,
    )
    ck, cv = cap_t_ref[0].T, cap_t_ref[1].T
    sh_c[...] = jnp.concatenate([ck, cv[:, 128:192], cv[:, 0:128]], axis=1)
    greet_wait(everyone)

    send = Sender(ss, rs)
    round1 = [send(msg.at[p[0]], got1.at[dp], p) for p in dp_peers]
    swap = send(hid_ref.at[1 - xl], hid_own.at[xl], pair)
    near_r1 = send(hid_ref.at[xl], hid_all.at[1, xl], right)
    near_l1 = send(hid_ref.at[xl], hid_all.at[2, xl], left)
    ga = PlaneGather(send, sh_a, w_a)
    gc = PlaneGather(send, sh_c, w_c)
    gf = PlaneGather(send, sh_f, w_f)
    ga.start(local_sems.at[1])
    got1[dp] = msg[dp]
    sh_f[:, 0:512] = ffn_w_ref[0]
    sh_f[:, 512:1024] = ffn_w_ref[1]
    sh_f[:, 1024:1536] = down_t_ref[...]
    length = facts[LENGTH_ROW : LENGTH_ROW + 1, :]
    text_len = facts[TEXT_ROW : TEXT_ROW + 1, :]
    for copy in round1:
        copy.wait_recv()
    rows = got1[...].reshape(128, 128)[:, :64].astype(BF16)
    here = t == dp // 2
    low_bias = jnp.where(jnp.logical_and(here, dp % 2 == 0), 1.0, 0.0)
    high_bias = jnp.where(jnp.logical_and(here, dp % 2 == 1), 1.0, 0.0)
    terms = mm(rows, ada_ref[...])
    bias = [facts[BIAS_ROW + j : BIAS_ROW + j + 1, :] for j in range(3)]
    bias = [row * low_bias for row in bias] + [row * high_bias for row in bias]
    for d in range(16):
        for j in range(6):
            sent2[d, 2 * j : 2 * j + 2, :] = terms[8 * d : 8 * d + 2, 128 * j : 128 * j + 128] + bias[j]
    round2 = [send(sent2.at[p[0]], got2.at[dp], p) for p in dp_peers]
    got2[dp] = sent2[dp]
    load_hid.wait()
    swap.wait_recv()
    near_r2 = send(hid_own.at[1 - xl], hid_all.at[1, 1 - xl], right)
    near_l2 = send(hid_own.at[1 - xl], hid_all.at[2, 1 - xl], left)
    hid_all[0] = hid_own[...]
    for copy in round2:
        copy.wait_recv()
    got3[t] = jnp.sum(got2[...], axis=0)
    round3 = [send(got3.at[t], got3.at[t], p) for p in t_peers]
    ga.step3()
    gc.start(local_sems.at[2])
    fill_rope(
        cos_ref,
        sin_ref,
        z,
        length,
        facts[FRAMES_ROW : FRAMES_ROW + 1, :],
        facts[WIDTH_ROW : WIDTH_ROW + 1, :],
    )
    flush(cos_ref, cos_out)
    flush(sin_ref, sin_out)
    near_r1.wait_recv()
    near_r2.wait_recv()
    far_r = send(hid_all.at[1, 0], hid_all.at[3, 0], right)
    near_l1.wait_recv()
    near_l2.wait_recv()
    far_l = send(hid_all.at[2, 1], hid_all.at[3, 1], left)
    for d in range(16):
        gains_ref[0:4, d * 96 : (d + 1) * 96] = got1[d, 4:8, 0:96]
    gains_ref[4:8, :] = jnp.zeros((4, D), F32)
    slot_row = lax.broadcasted_iota(jnp.int32, (128, 128), 0) + z * 128
    live_ref[...] = jnp.where(slot_row.astype(F32) < length, 1.0, 0.0)
    for copy in round3:
        copy.wait_recv()
    for i in range(4):
        for h in range(2):
            block = got3[2 * i + h]
            for j in range(6):
                lo = h * 768 + j * 128
                mod_ref[i : i + 1, lo : lo + 128] = jnp.where(
                    xl == 0, block[2 * j : 2 * j + 1], block[2 * j + 1 : 2 * j + 2]
                )
    mod_ref[4:8, :] = jnp.zeros((4, D), F32)
    factor = gains_ref[0:1, :] * (1.0 + mod_ref[0:1, :])

    def scale_rows(slot, carry):
        unit_rows, _ = normalize(hid_all[slot].reshape(128, D).astype(F32))
        first[slot] = (unit_rows * factor).astype(BF16)
        return carry

    load_cap.wait()

    def flip_caption(j, carry):
        rows = tile(j, 128)
        cap_flip[rows, 0:128] = cap[0:128, rows].T
        cap_flip[rows, 128:256] = cap[128:256, rows].T
        return carry

    lax.fori_loop(0, 3, scale_rows, 0)
    ga.step4()
    far_r.wait_recv()
    far_l.wait_recv()
    scale_rows(3, 0)
    resid_ref[...] = hid_all[0].reshape(128, D)
    flush(resid_ref, resid_out)
    gc.step3()
    gf.start(local_sems.at[3])
    transpose_into(first, first_flip)
    flush(first_flip, first_flip_out)
    lax.fori_loop(0, 32, flip_caption, 0)
    flush(cap_flip, cap_flip_out)
    ga.step5()
    ga.finish()
    flush(w_a, w_a_out)

    x_rows = first[...].reshape(512, D)
    low_head = lanes((512, 128)) < 64

    def project(xx, cols):
        w_cols = w_a[xx, :, :, :, :, cols].reshape(D, cols.stop - cols.start)
        return mm(x_rows, w_cols)

    def project_side(xx, carry):
        p = project(xx, slice(0, 256))
        qr[xx] = p[:, :128].reshape(4, 128, 128)
        mixed[0, xx] = p[:, 128:]
        p = project(xx, slice(256, 512))
        kr[xx] = p[:, :128].reshape(4, 128, 128)
        vv[xx] = p[:, 128:].astype(BF16).reshape(4, 128, 128)
        mixed[1, xx] = project(xx, slice(512, 640))
        return carry

    lax.fori_loop(0, 2, project_side, 0)
    x0, x1 = mixed[0, 0], mixed[0, 1]
    qr[2] = jnp.where(low_head, x0, pltpu.roll(x1, 64, 1)).reshape(4, 128, 128)
    kr[2] = jnp.where(low_head, pltpu.roll(x0, 64, 1), x1).reshape(4, 128, 128)
    x0, x1 = mixed[1, 0], mixed[1, 1]
    vv[2] = jnp.where(low_head, x0, pltpu.roll(x1, 64, 1)).astype(BF16).reshape(4, 128, 128)
    block = head_block()
    cos = cos_ref[...].reshape(512, 128)
    sin = sin_ref[...].reshape(512, 128)

    def turned(raw, gain):
        raw = raw.reshape(512, 128)
        v = raw * lax.rsqrt(head_mean(raw * raw, block) + EPSILON) * gain
        return v * cos + swap_quarters(v) * sin

    for p in range(3):
        q = turned(qr[p], facts[GAIN_ROW : GAIN_ROW + 1, :]).astype(BF16)
        q8[p] = (q.astype(F32) * 0.125).astype(BF16).reshape(4, 128, 128)
        k = turned(kr[p], facts[GAIN_ROW + 1 : GAIN_ROW + 2, :])
        kk[p] = k.astype(BF16).reshape(4, 128, 128)
    for src, dst in ((q8, q8_out), (kk, kk_out), (vv, vv_out), (qr, qr_out), (kr, kr_out)):
        flush(src, dst)

    self_bias = key_bias(512, z, length)
    text_bias = key_bias(256, z, text_len)
    lse_ref[...] = jnp.zeros((4, 128, 128), F32)

    def attend_rows(p, text, b):
        slots = pl.ds(b * 2, 2)
        q = q8[p, slots].reshape(256, 128)
        k = tk[p] if text else kk[p].reshape(512, 128)
        v = tv[p] if text else vv[p].reshape(512, 128)
        low_rows = lanes((256, 128)) < 64
        mix = jnp.zeros((256, 128), F32)
        for head in range(2):
            keep = low_rows if head == 0 else jnp.logical_not(low_rows)
            qm = jnp.where(keep, q, jnp.zeros_like(q))
            scores = mm_t(qm, k) + (text_bias if text else self_bias)
            top = jnp.max(scores, axis=-1, keepdims=True)
            e = jnp.exp(scores - top)
            total = jnp.sum(e, axis=-1, keepdims=True)
            probs = (e * (1.0 / total)).astype(BF16)
            mix = mix + jnp.where(keep, mm(probs, v), 0.0)
            here = lanes((256, 128)) == p * 2 + head + 8 * text
            old = lse_ref[slots].reshape(256, 128)
            lse_ref[slots] = jnp.where(here, top + jnp.log(total), old).reshape(2, 128, 128)
        if not text:
            own_ref[p, slots] = mix.reshape(2, 128, 128)
            return
        other_ref[p, slots] = mix.reshape(2, 128, 128)
        gate = facts[pl.ds(GATE_ROW + p, 1), :]
        both = own_ref[p, slots].reshape(256, 128) + gate * mix
        own_ref[p, slots] = both.reshape(2, 128, 128)

    def attend(lo, hi, text):
        def step(i, carry):
            attend_rows(i // 2, text, i % 2)
            return carry

        lax.fori_loop(2 * lo, 2 * hi, step, 0)

    attend(0, 1, False)
    gc.step4()
    gf.step3()
    cot_swap = send(cot_ref.at[1 - xl], cot_out.at[xl], pair)
    attend(1, 3, False)
    gc.step5()
    gc.finish()
    low_text = lanes((256, 128)) < 64

    def text_side(xx, carry):
        total = mm(cap[:, 0:2048], w_c[xx, 0].reshape(2048, 384))
        total = total + mm(cap[:, 2048:4096], w_c[xx, 1].reshape(2048, 384))
        tkr[xx] = total[:, 0:128]
        tv[xx] = total[:, 256:384].astype(BF16)
        mixed[0, xx, 0:256, :] = total[:, 128:256]
        return carry

    lax.fori_loop(0, 2, text_side, 0)
    x0, x1 = mixed[0, 0, 0:256, :], mixed[0, 1, 0:256, :]
    tkr[2] = jnp.where(low_text, x0, pltpu.roll(x1, 64, 1))
    tv[2] = jnp.where(low_text, pltpu.roll(x0, 64, 1), x1).astype(BF16)
    flush(tv, tv_out)
    for p in range(3):
        raw = tkr[p]
        gain = facts[GAIN_ROW + 2 : GAIN_ROW + 3, :]
        tk[p] = (raw * lax.rsqrt(head_mean(raw * raw, block) + EPSILON) * gain).astype(BF16)
    flush(tkr, tkr_out)
    flush(tk, tk_out)
    attend(0, 3, True)
    for p in range(2):
        cw[p, :, :, 128:256] = own_ref[p].astype(BF16)
    both = own_ref[2].reshape(512, 128)
    zero = jnp.zeros_like(both)
    moved = pltpu.roll(both, 64, 1)
    cw[0, :, :, 0:128] = jnp.where(low_head, zero, moved).astype(BF16).reshape(4, 128, 128)
    cw[1, :, :, 0:128] = jnp.where(low_head, zero, both).astype(BF16).reshape(4, 128, 128)
    flush(lse_ref, lse_out)
    flush(other_ref, other_out)
    flush(cw, cw_out)

    def out_rows(lo, count):
        n = count * 128
        a0 = cw[0, lo : lo + count].reshape(n, 256)
        a1 = cw[1, lo : lo + count].reshape(n, 256)
        def column(xb, carry):
            b0 = w_a[0, xb, :, :, :, 512:768].reshape(768, 256)
            b1 = w_a[1, xb, :, :, :, 512:768].reshape(768, 256)
            total = mm_t(a0, b0) + mm_t(a1, b1)
            part[lo : lo + count, :, tile(xb, 768)] = total.astype(BF16).reshape(count, 128, 768)
            return carry

        lax.fori_loop(0, 2, column, 0)

    sums = ZScatter(send, part, relay, got, right, left)
    out_rows(3, 1)
    sums.far()
    out_rows(1, 2)
    sums.near()
    out_rows(0, 1)
    gf.step4()
    sums.pass_on()
    gf.step5()
    attn = sums.total()
    attn_ref[...] = attn
    flush(attn_ref, attn_out)
    unit_two, _ = normalize(attn)
    live = live_ref[...][:, :1]
    middle = resid_ref[...].astype(F32) + live * jnp.tanh(mod_ref[1:2, :]) * unit_two * gains_ref[1:2, :]
    mid_ref[...] = middle
    flush(mid_ref, mid_out)
    unit_three, _ = normalize(middle)
    second_ref[...] = (unit_three * gains_ref[2:3, :] * (1.0 + mod_ref[2:3, :])).astype(BF16)
    flush(second_ref, second_out)
    cot_swap.wait_recv()
    gf.finish()
    send.drain()
    for copy in flushes:
        copy.wait()


def attention_call(args, cid):
    S = jax.ShapeDtypeStruct
    vm = pl.BlockSpec(memory_space=VMEM)
    any_ = pl.BlockSpec(memory_space=pl.ANY)
    pair = (3, 4, 128, 128)
    saved = [
        ((2, 2, 4, 2, 96, 768), BF16),
        ((4096, 256), BF16),
        ((D, 512), BF16),
        (pair, BF16),
        (pair, BF16),
        (pair, BF16),
        (pair, F32),
        (pair, F32),
        ((3, 256, 128), F32),
        (pair, F32),
        ((4, 128, 128), F32),
        ((2, 4, 128, 256), BF16),
        ((4, 128, 128), F32),
        ((4, 128, 128), F32),
        ((128, D), BF16),
        ((3, 256, 128), BF16),
        ((3, 256, 128), BF16),
        ((128, D), F32),
        ((128, D), F32),
        ((128, D), BF16),
    ]
    outs = [
        ((8, D), F32),
        ((8, D), F32),
        ((16, 8, 128), F32),
        ((128, 128), F32),
        ((16, 128), F32),
    ]
    return pl.pallas_call(
        attention_kernel,
        out_shape=[S((2, 2, 4, 2, 96, D), BF16)]
        + [S(*o) for o in saved]
        + [S((2, 64, D), BF16)]
        + [S(*o) for o in outs],
        in_specs=[any_] * 3 + [vm] * 15,
        out_specs=[any_] * (2 + len(saved)) + [vm] * len(outs),
        scratch_shapes=[VMEM(*o) for o in saved]
        + [
            VMEM((4, 128, D), BF16),
            VMEM(pair, F32),
            VMEM((96, 768), BF16),
            VMEM((96, D), BF16),
            VMEM((256, 384), BF16),
            VMEM((2, 2, 4, 2, 256, 384), BF16),
            VMEM((256, 4096), BF16),
            VMEM((4, 2, 64, D), BF16),
            VMEM((2, 64, D), BF16),
            VMEM((16, 8, 128), F32),
            VMEM((16, 16, 128), F32),
            VMEM((16, 16, 128), F32),
            VMEM((8, 16, 128), F32),
            VMEM((2, 2, 512, 128), F32),
            VMEM((4, 128, D), BF16),
            VMEM((2, 64, D), BF16),
            VMEM((2, 128, D), BF16),
            pltpu.SemaphoreType.DMA((28,)),
        ]
        + dma_sems(160),
        compiler_params=pltpu.CompilerParams(
            collective_id=cid, has_side_effects=True, vmem_limit_bytes=58 * 2**20
        ),
        name="attention",
    )(*args)


def ffn_kernel(
    x_ref,
    w_hbm,
    mid_in,
    attn_in,
    cot_in,
    mod_ref,
    gain_ref,
    live_ref,
    out_out,
    gmid_out,
    gattn_out,
    dw_half,
    sums_ref,
    mid_ref,
    attn_ref,
    cot_ref,
    out_ref,
    gmid_ref,
    gattn_ref,
    w,
    dw_ref,
    dw_got,
    x_all,
    g_all,
    act,
    dgate,
    dup,
    gpre,
    part1,
    part2,
    relay1,
    relay2,
    got1,
    got2,
    flip,
    flip_g,
    own_g,
    w_sem,
    out_sems,
    ss,
    rs,
):
    z, right, left = z_ring()
    load = pltpu.make_async_copy(w_hbm, w, w_sem)
    load.start()
    loads = []
    for src, dst in ((x_ref, x_all.at[0]), (mid_in, mid_ref), (attn_in, attn_ref), (cot_in, cot_ref)):
        copy = pltpu.make_async_copy(src, dst, out_sems.at[4 + len(loads)])
        copy.start()
        loads.append(copy)
    stores = []

    def store(src, dst):
        copy = pltpu.make_async_copy(src, dst, out_sems.at[8 + len(stores)])
        copy.start()
        stores.append(copy)

    xh, xl, y, _, c = coords()
    sibling = device_of(2 * xh + xl, y, z, 1 - c)
    greet([right, left, sibling])
    send = Sender(ss, rs)
    one = ZGather(send, x_ref, x_all, right, left)
    for copy in loads:
        copy.wait()
    load.wait()

    def pre(lo, count):
        rows = count * 128
        x = x_all[lo : lo + count].reshape(rows, D)

        def column(i, carry):
            xx, j = i // 2, i % 2
            g = mm(x, w[xx, :, tile(j)])
            u = mm(x, w[xx, :, tile(j + 2)])
            s = jax.nn.sigmoid(g)
            gs = g * s
            act[xx, lo : lo + count, :, tile(j)] = (gs * u).astype(BF16).reshape(count, 128, 256)
            dgate[xx, lo : lo + count, :, tile(j)] = (u * s * (1.0 + g * (1.0 - s))).reshape(count, 128, 256)
            dup[xx, lo : lo + count, :, tile(j)] = gs.reshape(count, 128, 256)
            return carry

        lax.fori_loop(0, 4, column, 0)

    def down(lo, count):
        rows = count * 128
        a0 = act[0, lo : lo + count].reshape(rows, 512)
        a1 = act[1, lo : lo + count].reshape(rows, 512)

        def column(j, carry):
            cols = tile(j)
            total = mm_t(a0, w[0, cols, 1024:1536]) + mm_t(a1, w[1, cols, 1024:1536])
            part1[lo : lo + count, :, cols] = total.astype(BF16).reshape(count, 128, 256)
            return carry

        lax.fori_loop(0, D // 256, column, 0)

    sum1 = ZScatter(send, part1, relay1, got1, right, left)
    pre(0, 1)
    one.near()
    pre(1, 2)
    down(1, 2)
    sum1.near()
    one.far()
    pre(3, 1)
    down(3, 1)
    sum1.far()
    down(0, 1)
    transpose_into(x_all, flip)
    sum1.pass_on()
    ffn_total = sum1.total()

    live = live_ref[...][:, :1]
    mod = mod_ref[...]
    gains = gain_ref[...]
    gate_f = jnp.tanh(mod[3:4])
    middle = mid_ref[...]
    unit_four, inverse_four = normalize(ffn_total)
    out_ref[...] = (middle + live * gate_f * unit_four * gains[3:4]).astype(BF16)
    store(out_ref, out_out)
    grad_top = cot_ref[...].astype(F32)
    weighted = grad_top * live
    part_four = jnp.sum(weighted * unit_four, axis=0, keepdims=True)
    own_g[...] = norm_back(unit_four, inverse_four, weighted * gate_f * gains[3:4]).astype(BF16)
    two = ZGather(send, own_g, g_all, right, left)
    g_all[0] = own_g[...]
    sums_ref[3:4, :] = part_four * gains[3:4] * (1.0 - gate_f * gate_f)
    sums_ref[7:8, :] = part_four * gate_f

    def back(lo, count):
        rows = count * 128
        g = g_all[lo : lo + count].reshape(rows, D)

        def column(i, carry):
            xx, j = i // 2, i % 2
            ga = mm(g, w[xx, :, tile(j + 4)])
            dg = dgate[xx, lo : lo + count, :, tile(j)].reshape(rows, 256)
            du = dup[xx, lo : lo + count, :, tile(j)].reshape(rows, 256)
            gpre[xx, lo : lo + count, :, tile(j)] = (ga * dg).astype(BF16).reshape(count, 128, 256)
            gpre[xx, lo : lo + count, :, tile(j + 2)] = (ga * du).astype(BF16).reshape(count, 128, 256)
            return carry

        lax.fori_loop(0, 4, column, 0)

    def back_in(lo, count):
        rows = count * 128
        a0 = gpre[0, lo : lo + count].reshape(rows, 1024)
        a1 = gpre[1, lo : lo + count].reshape(rows, 1024)

        def column(j, carry):
            cols = tile(j)
            total = mm_t(a0, w[0, cols, 0:1024]) + mm_t(a1, w[1, cols, 0:1024])
            part2[lo : lo + count, :, cols] = total.astype(BF16).reshape(count, 128, 256)
            return carry

        lax.fori_loop(0, D // 256, column, 0)

    def weight_grad(xx):
        def column(i, carry):
            j, xb = i // 2, i % 2
            b = gpre[xx, :, :, tile(j)].reshape(512, 256)
            grad = mm(flip[tile(xb, 768), :], b)
            dw_ref[xx, xb, :, :, :, tile(j)] = grad.astype(BF16).reshape(4, 2, 96, 256)
            return carry

        lax.fori_loop(0, 8, column, 0)

        def down_column(i, carry):
            j, xb = i // 2, i % 2
            b = act[xx, :, :, tile(j)].reshape(512, 256)
            grad = mm(flip_g[tile(xb, 768), :], b)
            dw_ref[xx, xb, :, :, :, tile(j + 4)] = grad.astype(BF16).reshape(4, 2, 96, 256)
            return carry

        lax.fori_loop(0, 4, down_column, 0)
        return [
            send(dw_ref.at[xx, xb, :, 1 - c], dw_got.at[xx, xb], sibling) for xb in range(2)
        ]

    def add_sibling(xx, copies):
        for xb in range(2):
            copies[xb].wait_recv()

            def add(j, carry, xb=xb):
                dw_got[xx, xb, j] = add_low(dw_got[xx, xb, j], dw_ref[xx, xb, j, c])
                return carry

            lax.fori_loop(0, 4, add, 0)
            store(dw_got.at[xx, xb], dw_half.at[xx, xb])

    sum2 = ZScatter(send, part2, relay2, got2, right, left)
    back(0, 1)
    two.near()
    back(1, 2)
    back_in(1, 2)
    sum2.near()
    two.far()
    back(3, 1)
    back_in(3, 1)
    sum2.far()
    back_in(0, 1)
    transpose_into(g_all, flip_g)
    to_sibling0 = weight_grad(0)
    sum2.pass_on()
    to_sibling1 = weight_grad(1)
    add_sibling(0, to_sibling0)
    grad_second = sum2.total()

    scale_f = mod[2:3]
    unit_three, inverse_three = normalize(middle)
    sum_three = jnp.sum(grad_second * unit_three, axis=0, keepdims=True)
    sums_ref[2:3, :] = sum_three * gains[2:3]
    sums_ref[6:7, :] = sum_three * (1.0 + scale_f)
    grad_middle = grad_top + norm_back(
        unit_three, inverse_three, grad_second * (1.0 + scale_f) * gains[2:3]
    )
    gmid_ref[...] = grad_middle
    store(gmid_ref, gmid_out)
    gate_a = jnp.tanh(mod[1:2])
    unit_two, inverse_two = normalize(attn_ref[...])
    weighted_mid = grad_middle * live
    sum_two = jnp.sum(weighted_mid * unit_two, axis=0, keepdims=True)
    sums_ref[1:2, :] = sum_two * gains[1:2] * (1.0 - gate_a * gate_a)
    sums_ref[5:6, :] = sum_two * gate_a
    sums_ref[0:1, :] = jnp.zeros((1, D), F32)
    sums_ref[4:5, :] = jnp.zeros((1, D), F32)
    gattn_ref[...] = norm_back(unit_two, inverse_two, weighted_mid * gate_a * gains[1:2]).astype(BF16)
    store(gattn_ref, gattn_out)
    add_sibling(1, to_sibling1)
    send.drain()
    for copy in stores:
        copy.wait()


def ffn_call(second_in, w_f, middle, attn, cot, mod_rows, gains, live, cid):
    S = jax.ShapeDtypeStruct
    vm = pl.BlockSpec(memory_space=VMEM)
    any_ = pl.BlockSpec(memory_space=pl.ANY)
    return pl.pallas_call(
        ffn_kernel,
        out_shape=[
            S((128, D), BF16),
            S((128, D), F32),
            S((128, D), BF16),
            S((2, 2, 4, 96, D), BF16),
            S((8, D), F32),
        ],
        in_specs=[any_] * 5 + [vm] * 3,
        out_specs=[any_] * 4 + [vm],
        scratch_shapes=[
            VMEM((128, D), F32),
            VMEM((128, D), F32),
            VMEM((128, D), BF16),
            VMEM((128, D), BF16),
            VMEM((128, D), F32),
            VMEM((128, D), BF16),
            VMEM((2, D, D), BF16),
            VMEM((2, 2, 4, 2, 96, D), BF16),
            VMEM((2, 2, 4, 96, D), BF16),
            VMEM((4, 128, D), BF16),
            VMEM((4, 128, D), BF16),
            VMEM((2, 4, 128, 512), BF16),
            VMEM((2, 4, 128, 512), F32),
            VMEM((2, 4, 128, 512), F32),
            VMEM((2, 4, 128, 1024), BF16),
            VMEM((4, 128, D), BF16),
            VMEM((4, 128, D), BF16),
            VMEM((2, 64, D), BF16),
            VMEM((2, 64, D), BF16),
            VMEM((2, 128, D), BF16),
            VMEM((2, 128, D), BF16),
            VMEM((D, 512), BF16),
            VMEM((D, 512), BF16),
            VMEM((128, D), BF16),
            pltpu.SemaphoreType.DMA,
            pltpu.SemaphoreType.DMA((16,)),
        ]
        + dma_sems(40),
        compiler_params=pltpu.CompilerParams(
            collective_id=cid, has_side_effects=True, vmem_limit_bytes=56 * 2**20
        ),
        name="ffn",
    )(second_in, w_f, middle, attn, cot, mod_rows, gains, live)


def pick(array, index):
    return lax.dynamic_index_in_dim(array, index, 0, keepdims=False)


def dot(spec, a, b):
    return jnp.einsum(spec, a, b, preferred_element_type=F32)


class PlaneScatter:
    def __init__(self, send, grads, own, bufs):
        self.send, self.grads, self.own = send, grads, own
        self.sib, self.ra, self.rb, self.ga, self.gb, self.ha, self.hb = bufs
        rows, cols = self.sib.shape[3:]
        self.rows, self.cols = rows, cols
        self.half = half = rows // 2
        self.top, self.low = pl.ds(0, half), pl.ds(half, half)
    def setup(self):
        self.where = plane_peers()
        self.go_xr, self.go_xq, self.go_yr, self.go_yq, self.sibling, self.go_xo, self.go_yo = self.where[7]
        self.parts = {}

    def to_sibling(self, k):
        block = self.grads.at[k % 2, k // 2]
        if self.own is None:
            block = self.grads.at[k % 2, k // 2, :, 1 - self.where[2]]
        self.parts[k] = self.send(block, self.sib.at[k % 2, k // 2], self.sibling)

    def add(self):
        c, sib, own, grads = self.where[2], self.sib, self.own, self.grads
        for k in self.parts:
            self.parts[k].wait_recv()

            def add_sibling(j, carry, k=k):
                if own is None:
                    mine = grads[k % 2, k // 2, j, c]
                else:
                    mine = own(k % 2, k // 2, j)
                sib[k % 2, k // 2, j] = add_low(sib[k % 2, k // 2, j], mine)
                return carry

            lax.fori_loop(0, 4, add_sibling, 0)

    def first(self):
        x, y, c, xr, xq, yr, yq, _ = self.where
        sib, send = self.sib, self.send
        xo, yo = (x + 2) % 4, (y + 2) % 4
        self.t1 = send(sib.at[0, :, yo, self.top], self.ra.at[pl.ds(0, 2)], self.go_yr)
        self.t2 = send(sib.at[1, :, yo, self.top], self.ra.at[pl.ds(2, 2)], self.go_yq)
        self.l1 = send(sib.at[xo % 2, xo // 2, pl.ds(0, 2), self.low], self.rb.at[pl.ds(0, 2)], self.go_xr)
        self.l2 = send(sib.at[xo % 2, xo // 2, pl.ds(2, 2), self.low], self.rb.at[pl.ds(2, 2)], self.go_xq)

    def step2(self):
        x, y, c, xr, xq, yr, yq, _ = self.where
        sib, send, top, low = self.sib, self.send, self.top, self.low
        ra, rb = self.ra, self.rb
        self.t1.wait_recv()
        for j in range(2):
            sib[0, j, yr, top] = add_low(sib[0, j, yr, top], ra[j])
        self.t3 = send(sib.at[:, :, yr, top], self.ga.at[0], self.go_yr)
        self.t2.wait_recv()
        for j in range(2):
            sib[1, j, yq, top] = add_low(sib[1, j, yq, top], ra[2 + j])
        self.t4 = send(sib.at[:, :, yq, top], self.ga.at[1], self.go_yq)
        self.l1.wait_recv()
        for j in range(2):
            sib[xr % 2, xr // 2, j, low] = add_low(sib[xr % 2, xr // 2, j, low], rb[j])
        self.l3 = send(sib.at[xr % 2, xr // 2, :, low], self.gb.at[0], self.go_xr)
        self.l2.wait_recv()
        for j in range(2):
            sib[xq % 2, xq // 2, 2 + j, low] = add_low(sib[xq % 2, xq // 2, 2 + j, low], rb[2 + j])
        self.l4 = send(sib.at[xq % 2, xq // 2, :, low], self.gb.at[1], self.go_xq)

    def step3(self):
        x, y, c, xr, xq, yr, yq, _ = self.where
        sib, send, ga, gb, pa, pb = self.sib, self.send, self.ga, self.gb, self.ra, self.rb
        xo, yo = (x + 2) % 4, (y + 2) % 4
        self.t3.wait_recv()
        self.t4.wait_recv()
        for i in range(2):
            for j in range(2):
                total = sib[i, j, y, self.top].astype(F32) + ga[0, i, j].astype(F32)
                pa[2 * j + i] = (total + ga[1, i, j].astype(F32)).astype(BF16)
        ha, hb = self.ha, self.hb
        self.last_a = [
            send(pa.at[xr], ha.at[0], self.go_xr),
            send(pa.at[xq], ha.at[1], self.go_xq),
            send(pa.at[xo], ha.at[2], self.go_xo),
        ]
        self.l3.wait_recv()
        self.l4.wait_recv()
        for j in range(4):
            total = sib[x % 2, x // 2, j, self.low].astype(F32) + gb[0, j].astype(F32)
            pb[j] = (total + gb[1, j].astype(F32)).astype(BF16)
        self.last_b = [
            send(pb.at[yr], hb.at[0], self.go_yr),
            send(pb.at[yq], hb.at[1], self.go_yq),
            send(pb.at[yo], hb.at[2], self.go_yo),
        ]

    def finish(self):
        x, y = self.where[:2]
        results = []
        for copies, mine, got in (
            (self.last_a, self.ra[x], self.ha),
            (self.last_b, self.rb[y], self.hb),
        ):
            for copy in copies:
                copy.wait_recv()
            total = mine.astype(F32) + got[0].astype(F32)
            results.append(total + got[1].astype(F32) + got[2].astype(F32))
        return results


def scatter_bufs(rows, cols):
    half = rows // 2
    return [
        VMEM((2, 2, 4, rows, cols), BF16),
        VMEM((4, half, cols), BF16),
        VMEM((4, half, cols), BF16),
        VMEM((2, 2, 2, half, cols), BF16),
        VMEM((2, 4, half, cols), BF16),
        VMEM((3, half, cols), BF16),
        VMEM((3, half, cols), BF16),
    ]


def mm_rows(a, b):
    return lax.dot_general(a, b, (((0,), (0,)), ((), ())), preferred_element_type=F32)


def back_kernel(
    sib_in,
    w_a_in,
    cap_flip_in,
    first_flip_in,
    q8_in,
    kk_in,
    vv_in,
    qr_in,
    kr_in,
    tkr_in,
    other_in,
    lse_in,
    cw_in,
    cos_in,
    sin_in,
    resid_in,
    tk_in,
    tv_in,
    gmid_in,
    gattn_in,
    out_ref,
    mod_ref,
    gains_ref,
    sums_ref,
    facts,
    d_final,
    f_final,
    c_final,
    layer_final,
    hidden_final,
    g_all,
    gain_out,
    sib_f,
    w_a,
    cap_flip,
    first_flip,
    q8,
    kk,
    vv,
    qr,
    kr,
    tkr,
    other_ref,
    lse_ref,
    cw,
    cos_ref,
    sin_ref,
    resid_ref,
    tk,
    tv,
    gmid_ref,
    d_out,
    f_out,
    c_out,
    flip,
    grad_all,
    gc,
    gq,
    gk,
    gv,
    gtk,
    gtv,
    gpack,
    tpack,
    dw_a,
    dw_c,
    part,
    relay,
    got,
    hid_grad,
    mod_msg,
    gain_msg,
    got_mod,
    got_gain,
    gain_sum,
    sf1, sf2, sf3, sf4, sf5, sf6,
    sa0, sa1, sa2, sa3, sa4, sa5, sa6,
    sc0, sc1, sc2, sc3, sc4, sc5, sc6,
    local_sems,
    ss,
    rs,
):
    dp = lax.axis_index("dp")
    t = lax.axis_index("tensor")
    xh, xl, y, z, c = coords()
    _, right, left = z_ring()
    pair = device_of(2 * xh + 1 - xl, y, z, c)
    dp_peers = [((dp + k) % 16, t) for k in range(1, 16)]
    t_peers = [(dp, (t + k) % 8) for k in range(1, 8)]
    outer_x = device_of((2 * xh + xl + 3 - 2 * xl) % 4, y, z, c)
    everyone = dp_peers + t_peers + [outer_x]
    greet_signal(everyone)
    loads = []
    for src, dst in (
        (sib_in, sib_f),
        (w_a_in, w_a),
        (q8_in, q8),
        (gattn_in, grad_all.at[0]),
        (tk_in, tk),
        (tv_in, tv),
        (kk_in, kk),
        (vv_in, vv),
        (lse_in, lse_ref),
        (tkr_in, tkr),
        (cap_flip_in, cap_flip),
        (cw_in, cw),
        (qr_in, qr),
        (kr_in, kr),
        (cos_in, cos_ref),
        (sin_in, sin_ref),
        (other_in, other_ref),
        (first_flip_in, first_flip),
        (resid_in, resid_ref),
        (gmid_in, gmid_ref),
    ):
        copy = pltpu.make_async_copy(src, dst, local_sems.at[len(loads)])
        copy.start()
        loads.append(copy)
    greet_wait(everyone)
    send = Sender(ss, rs)
    tokens = ZGather(send, gattn_in, grad_all, right, left)

    def caption_own(xx, xb, yb):
        return mm(cap_flip[tile(2 * (4 * xb + yb) + c)], tpack[xx])

    scat_f = PlaneScatter(send, None, None, (sib_f, sf1, sf2, sf3, sf4, sf5, sf6))
    scat_a = PlaneScatter(send, dw_a, None, (sa0, sa1, sa2, sa3, sa4, sa5, sa6))
    scat_c = PlaneScatter(send, dw_c, caption_own, (sc0, sc1, sc2, sc3, sc4, sc5, sc6))
    for scatter in (scat_f, scat_a, scat_c):
        scatter.setup()
    loads[0].wait()
    scat_f.first()
    stores = []

    def store(src, dst):
        copy = pltpu.make_async_copy(src, dst, local_sems.at[len(loads) + len(stores)])
        copy.start()
        stores.append(copy)

    store(out_ref.at[xl], layer_final.at[xl])
    out_swap = send(out_ref.at[1 - xl], layer_final.at[xl], pair)
    self_bias = key_bias(512, z, facts[LENGTH_ROW : LENGTH_ROW + 1, :])
    text_bias = key_bias(256, z, facts[TEXT_ROW : TEXT_ROW + 1, :])
    block = head_block()
    low_row = lanes((1, 128)) < 64
    gtk[...] = jnp.zeros((3, 256, 128), F32)
    gtv[...] = jnp.zeros((3, 256, 128), F32)
    gk[...] = jnp.zeros((3, 512, 128), F32)
    gv[...] = jnp.zeros((3, 512, 128), F32)
    for copy in loads[1:4]:
        copy.wait()

    def head_grads(lo, count):
        n = count * 128
        g = grad_all[lo : lo + count].reshape(n, D)
        low_lane = lanes((n, 128)) < 64
        tiles = []
        for xx in range(2):
            w_cols = w_a[xx, :, :, :, :, 512:768].reshape(D, 256)
            o = mm(g, w_cols)
            gc[xx, lo : lo + count] = o[:, 128:].astype(BF16).reshape(count, 128, 128)
            tiles.append(o[:, :128])
        both = jnp.where(low_lane, pltpu.roll(tiles[0], 64, 1), tiles[1])
        gc[2, lo : lo + count] = both.astype(BF16).reshape(count, 128, 128)

    def back_rows(p, lo, count, kinds):
        n = count * 128
        q = q8[p, lo : lo + count].reshape(n, 128)
        low_rows = lanes((n, 128)) < 64
        grad_q = jnp.zeros((n, 128), F32)
        for text in kinds:
            g = gc[p, lo : lo + count].reshape(n, 128)
            if text:
                g = (g.astype(F32) * facts[pl.ds(GATE_ROW + p, 1), :]).astype(BF16)
            k = tk[p] if text else kk[p].reshape(512, 128)
            v = tv[p] if text else vv[p].reshape(512, 128)
            to_v, to_k = (gtv, gtk) if text else (gv, gk)
            for head in range(2):
                keep = low_rows if head == 0 else jnp.logical_not(low_rows)
                qm = jnp.where(keep, q, jnp.zeros_like(q))
                gm = jnp.where(keep, g, jnp.zeros_like(g))
                here = lanes((n, 128)) == p * 2 + head + 8 * text
                kept = lse_ref[lo : lo + count].reshape(n, 128)
                lse = jnp.sum(jnp.where(here, kept, 0.0), axis=-1, keepdims=True)
                scores = mm_t(qm, k) + (text_bias if text else self_bias)
                probs = jnp.exp(scores - lse)
                grad_probs = mm_t(gm, v)
                delta = jnp.sum(probs * grad_probs, axis=-1, keepdims=True)
                grad_scores = (probs * (grad_probs - delta)).astype(BF16)
                grad_q = grad_q + jnp.where(keep, mm(grad_scores, k), 0.0)
                to_v[p] += mm_rows(probs.astype(BF16), gm)
                to_k[p] += mm_rows(grad_scores, qm)
        if 1 in kinds:
            gq[p, lo * 128 : lo * 128 + n] = grad_q
        else:
            gq[p, lo * 128 : lo * 128 + n] += grad_q

    def over_pairs(lo, count, kinds):
        def step(p, carry):
            back_rows(p, lo, count, kinds)
            return carry

        lax.fori_loop(0, 3, step, 0)

    head_grads(0, 1)
    for copy in loads[4:]:
        copy.wait()
    over_pairs(0, 1, (0, 1))
    tokens.near()
    head_grads(1, 2)
    scat_f.step2()
    over_pairs(1, 2, (1,))
    tokens.far()
    head_grads(3, 1)
    over_pairs(3, 1, (1,))

    def unit_of(raw):
        inverse = lax.rsqrt(head_mean(raw * raw, block) + EPSILON)
        return raw * inverse, inverse

    def back_head(unit, inverse, grad):
        return inverse * (grad - unit * head_mean(grad * unit, block))

    low_text = lanes((256, 128)) < 64
    text_row = jnp.zeros((1, 128), F32)
    grads_k = []
    for p in range(3):
        unit, inverse = unit_of(tkr[p])
        gtk_p = gtk[p]
        text_row = text_row + jnp.sum(gtk_p * unit, axis=0, keepdims=True)
        grads_k.append(back_head(unit, inverse, gtk_p * facts[GAIN_ROW + 2 : GAIN_ROW + 3, :]))
    for xx in range(2):
        tpack[xx, :, 0:128] = grads_k[xx].astype(BF16)
        tpack[xx, :, 256:384] = gtv[xx].astype(BF16)
    tpack[0, :, 128:256] = jnp.where(low_text, grads_k[2], pltpu.roll(gtv[2], 64, 1)).astype(BF16)
    tpack[1, :, 128:256] = jnp.where(low_text, pltpu.roll(grads_k[2], 64, 1), gtv[2]).astype(BF16)

    def caption_grad(i, carry):
        xx = i // 8
        j = i % 8
        grad = mm(cap_flip[tile(2 * j + 1 - c)], tpack[xx])
        dw_c[xx, j // 4, j % 4] = grad.astype(BF16)
        return carry

    lax.fori_loop(0, 8, caption_grad, 0)
    scat_c.to_sibling(0)
    scat_c.to_sibling(2)
    lax.fori_loop(8, 16, caption_grad, 0)
    scat_c.to_sibling(1)
    scat_c.to_sibling(3)
    transpose_into(grad_all, flip)
    over_pairs(1, 2, (0,))
    scat_f.step3()
    over_pairs(3, 1, (0,))
    scat_c.add()
    scat_c.first()
    cos = cos_ref[...].reshape(512, 128)
    sin = sin_ref[...].reshape(512, 128)
    low_head = lanes((512, 128)) < 64
    query_row = jnp.zeros((1, 128), F32)
    key_row = jnp.zeros((1, 128), F32)
    raws = [[], []]
    for p in range(3):
        for i in range(2):
            grad = (gq[p] * 0.125) if i == 0 else gk[p]
            raw = (qr if i == 0 else kr)[p].reshape(512, 128)
            turned = grad * cos - swap_quarters(grad) * sin
            unit, inverse = unit_of(raw)
            row = jnp.sum(turned * unit, axis=0, keepdims=True)
            if i == 0:
                query_row = query_row + row
            else:
                key_row = key_row + row
            result = back_head(unit, inverse, turned * facts[GAIN_ROW + i : GAIN_ROW + i + 1, :])
            if p < 2:
                gpack[p, :, (0 if i == 0 else 256) : (128 if i == 0 else 384)] = result.astype(BF16)
            else:
                raws[i] = result
    gpack[0, :, 128:256] = jnp.where(low_head, raws[0], pltpu.roll(raws[1], 64, 1)).astype(BF16)
    gpack[1, :, 128:256] = jnp.where(low_head, pltpu.roll(raws[0], 64, 1), raws[1]).astype(BF16)
    for xx in range(2):
        gpack[xx, :, 384:512] = gv[xx].astype(BF16)
    gpack[0, :, 512:640] = jnp.where(low_head, gv[2], 0.0).astype(BF16)
    gpack[1, :, 512:640] = jnp.where(low_head, pltpu.roll(gv[2], 64, 1), 0.0).astype(BF16)

    def first_rows(lo, count):
        n = count * 128
        a0 = gpack[0, lo * 128 : lo * 128 + n]
        a1 = gpack[1, lo * 128 : lo * 128 + n]
        def column(xb, carry):
            b0 = w_a[0, xb, :, :, :, 0:640].reshape(768, 640)
            b1 = w_a[1, xb, :, :, :, 0:640].reshape(768, 640)
            total = mm_t(a0, b0) + mm_t(a1, b1)
            part[lo : lo + count, :, tile(xb, 768)] = total.astype(BF16).reshape(count, 128, 768)
            return carry

        lax.fori_loop(0, 2, column, 0)

    def weight_grad(i, carry):
        xx, xb = i // 2, i % 2
        a = first_flip[tile(xb, 768)]
        g = flip[tile(xb, 768)]
        b = cw[xx].reshape(512, 256)
        grad = mm(a, gpack[xx, :, 0:512])
        dw_a[xx, xb, :, :, :, 0:512] = grad.astype(BF16).reshape(4, 2, 96, 512)
        grad = mm(g, b)
        last = grad[:, 0:128] + mm(a, gpack[xx, :, 512:640])
        dw_a[xx, xb, :, :, :, 512:640] = last.astype(BF16).reshape(4, 2, 96, 128)
        dw_a[xx, xb, :, :, :, 640:768] = grad[:, 128:256].astype(BF16).reshape(4, 2, 96, 128)
        return carry

    for xx in range(2):
        lax.fori_loop(2 * xx, 2 * xx + 2, weight_grad, 0)
        scat_a.to_sibling(xx)
        scat_a.to_sibling(xx + 2)
    scat_c.step2()
    sums = ZScatter(send, part, relay, got, right, left)
    first_rows(3, 1)
    sums.far()
    first_rows(1, 2)
    sums.near()
    scat_a.add()
    scat_a.first()
    first_rows(0, 1)
    sums.pass_on()
    scat_c.step3()
    scat_a.step2()
    top, low = scat_f.finish()
    f_out[0:48, :] = top
    f_out[48:96, :] = low
    store(f_out, f_final)

    grad_first = sums.total()

    unit_one, inverse_one = normalize(resid_ref[...].astype(F32))
    scale = 1.0 + mod_ref[0:1, :]
    gain = gains_ref[0:1, :]
    row_sum = jnp.sum(grad_first * unit_one, axis=0, keepdims=True)
    sums_0 = row_sum * gain
    sums_4 = row_sum * scale
    hid_grad[...] = (
        (gmid_ref[...] + norm_back(unit_one, inverse_one, grad_first * scale * gain))
        .astype(BF16)
        .reshape(2, 64, D)
    )
    grad_swap = send(hid_grad.at[1 - xl], hidden_final.at[xl], pair)
    store(hid_grad.at[xl], hidden_final.at[xl])
    mod_msg[...] = jnp.zeros((8, 8, 128), F32)
    gain_msg[...] = jnp.zeros((16, 16, 128), F32)
    for i in range(4):
        row = sums_0 if i == 0 else sums_ref[i : i + 1, :]
        for h in range(2):
            for j in range(6):
                lo = h * 768 + j * 128
                mod_msg[2 * i + h, j : j + 1, :] = row[:, lo : lo + 128]
    folded = [row + pltpu.roll(row, 64, 1) for row in (query_row, key_row, text_row)]
    first_line = jnp.where(low_row, folded[0], folded[1])
    lane = lanes((1, 128))
    second_line = jnp.where(low_row, folded[2], 0.0)
    for p in range(3):
        gate_row = facts[GATE_ROW + p : GATE_ROW + p + 1, :]
        products = gc[p].reshape(512, 128).astype(F32) * other_ref[p].reshape(512, 128)
        values = jnp.sum(products, axis=0, keepdims=True) * (1.0 - gate_row * gate_row)
        for head in range(2):
            keep = low_row if head == 0 else jnp.logical_not(low_row)
            value = jnp.sum(jnp.where(keep, values, 0.0), axis=1, keepdims=True)
            index = (0, 1, 3, 4, 2, 5)[2 * p + head]
            second_line = second_line + jnp.where(lane == 64 + z * 6 + index, value, 0.0)
    gain_rows = jnp.concatenate([sums_4, sums_ref[5:8, :]], axis=0)
    mod_rows = [sums_0] + [sums_ref[i : i + 1, :] for i in range(1, 4)]
    for d in range(16):
        for j in range(3):
            lo = (d % 4) * 384 + j * 128
            gain_msg[d, 8 + j : 9 + j, :] = mod_rows[d // 4][:, lo : lo + 128]
        gain_msg[d, 0:4, 0:96] = gain_rows[:, d * 96 : (d + 1) * 96]
        gain_msg[d, 4:5, :] = first_line
        gain_msg[d, 5:6, :] = second_line
    to_t = [send(mod_msg.at[q[1]], got_mod.at[t], q) for q in t_peers]
    to_dp = [send(gain_msg.at[q[0]], got_gain.at[dp], q) for q in dp_peers]
    got_mod[t] = mod_msg[t]
    got_gain[dp] = gain_msg[dp]
    scat_a.step3()
    for copy in to_t:
        copy.wait_recv()
    g_all[dp, 0] = got_mod[0] + got_mod[2] + got_mod[4] + got_mod[6]
    g_all[dp, 1] = got_mod[1] + got_mod[3] + got_mod[5] + got_mod[7]
    to_all = [send(g_all.at[dp], g_all.at[dp], q) for q in dp_peers]
    for copy in to_dp:
        copy.wait_recv()
    gain_sum[t] = jnp.sum(got_gain[...], axis=0)
    to_rest = [send(gain_sum.at[t], gain_sum.at[t], q) for q in t_peers]
    top, low = scat_a.finish()
    d_out[0:48, :] = top
    d_out[48:96, :] = low
    store(d_out, d_final)
    for copy in to_all + to_rest:
        copy.wait_recv()
    gain_out[...] = jnp.sum(gain_sum[...], axis=0)
    top, low = scat_c.finish()
    c_out[0:128, :] = top
    c_out[128:256, :] = low
    store(c_out, c_final)
    out_swap.wait_recv()
    grad_swap.wait_recv()
    send.drain()
    for copy in stores:
        copy.wait()


def back_call(args, cid):
    S = jax.ShapeDtypeStruct
    vm = pl.BlockSpec(memory_space=VMEM)
    any_ = pl.BlockSpec(memory_space=pl.ANY)
    loaded = args[:19]
    outs = [
        S((96, 768), F32),
        S((96, D), F32),
        S((256, 384), F32),
        S((2, 64, D), BF16),
        S((2, 64, D), BF16),
        S((16, 2, 8, 128), F32),
        S((16, 128), F32),
    ]
    return pl.pallas_call(
        back_kernel,
        out_shape=outs,
        in_specs=[any_] * 21 + [vm] * 4,
        out_specs=[any_] * 5 + [vm] * 2,
        scratch_shapes=[VMEM(a.shape, a.dtype) for a in loaded]
        + [
            VMEM((96, 768), F32),
            VMEM((96, D), F32),
            VMEM((256, 384), F32),
            VMEM((D, 512), BF16),
            VMEM((4, 128, D), BF16),
            VMEM((3, 4, 128, 128), BF16),
            VMEM((3, 512, 128), F32),
            VMEM((3, 512, 128), F32),
            VMEM((3, 512, 128), F32),
            VMEM((3, 256, 128), F32),
            VMEM((3, 256, 128), F32),
            VMEM((2, 512, 640), BF16),
            VMEM((2, 256, 384), BF16),
            VMEM((2, 2, 4, 2, 96, 768), BF16),
            VMEM((2, 2, 4, 256, 384), BF16),
            VMEM((4, 128, D), BF16),
            VMEM((2, 64, D), BF16),
            VMEM((2, 128, D), BF16),
            VMEM((2, 64, D), BF16),
            VMEM((8, 8, 128), F32),
            VMEM((16, 16, 128), F32),
            VMEM((8, 8, 128), F32),
            VMEM((16, 16, 128), F32),
            VMEM((8, 16, 128), F32),
        ]
        + scatter_bufs(96, D)[1:]
        + scatter_bufs(96, 768)
        + scatter_bufs(256, 384)
        + [pltpu.SemaphoreType.DMA((28,))]
        + dma_sems(140),
        compiler_params=pltpu.CompilerParams(
            collective_id=cid, has_side_effects=True, vmem_limit_bytes=62 * 2**20
        ),
        name="attention_back",
    )(*args)


def final_kernel(
    d_in,
    f_in,
    c_in,
    layer_in,
    hidden_in,
    g_in,
    gain_hbm,
    got_in,
    layer,
    hidden,
    ada,
    bias,
    gains,
    qkv,
    heads,
    cap,
    gate,
    out_w,
    ffn,
    down,
    d_ref,
    f_ref,
    c_ref,
    hidden_half,
    g_all,
    gain_in,
    got1,
    units,
    items,
    sems,
):
    loads = []
    for src, dst in (
        (layer_in, layer),
        (hidden_in, hidden_half),
        (got_in, got1),
        (g_in, g_all),
        (gain_hbm, gain_in),
        (d_in, d_ref),
        (f_in, f_ref),
        (c_in, c_ref),
    ):
        copy = pltpu.make_async_copy(src, dst, sems.at[len(loads)])
        copy.start()
        loads.append(copy)
    for copy in loads:
        copy.wait()
    hidden[...] = hidden_half[...].astype(F32)
    qkv[0] = d_ref[:, 0:192]
    qkv[1, :, 0:128] = d_ref[:, 256:384]
    qkv[1, :, 128:192] = d_ref[:, 192:256]
    qkv[2] = d_ref[:, 384:576]
    out_w[0:128, :] = d_ref[:, 640:768].T
    out_w[128:192, :] = d_ref[:, 576:640].T
    ffn[0] = f_ref[:, 0:512]
    ffn[1] = f_ref[:, 512:1024]
    down[...] = f_ref[:, 1024:1536]
    cap[0] = c_ref[:, 0:192].T
    cap[1, 0:128, :] = c_ref[:, 256:384].T
    cap[1, 128:192, :] = c_ref[:, 192:256].T
    for d in range(16):
        units[2 * d : 2 * d + 2, :] = got1[d, 0:2, 0:64]
        for j in range(6):
            items[2 * d : 2 * d + 2, j * 128 : j * 128 + 128] = jnp.concatenate(
                [g_all[d, 0, j : j + 1, :], g_all[d, 1, j : j + 1, :]], axis=0
            )
    unit_rows = units[...].astype(BF16)
    high = items[...].astype(BF16)
    low = (items[...] - high.astype(F32)).astype(BF16)
    ada[...] = mm_rows(unit_rows, high) + mm_rows(unit_rows, low)
    for j in range(3):
        bias[:, j * 128 : j * 128 + 128] = gain_in[8 + j : 9 + j, :]
    gains[...] = gain_in[0:4, 0:96]
    heads[0:1, :] = gain_in[4:5, 0:64]
    heads[1:2, :] = gain_in[4:5, 64:128]
    heads[2:3, :] = gain_in[5:6, 0:64]
    gate[...] = gain_in[5:6, 64:88]


def final_call(args):
    S = jax.ShapeDtypeStruct
    vm = pl.BlockSpec(memory_space=VMEM)
    outs = [
        S((2, 64, D), BF16),
        S((2, 64, D), F32),
        S((64, 768), F32),
        S((1, 384), F32),
        S((4, 96), F32),
        S((3, 96, 192), F32),
        S((3, 64), F32),
        S((2, 192, 256), F32),
        S((1, 24), F32),
        S((192, 96), F32),
        S((2, 96, 512), F32),
        S((96, 512), F32),
    ]
    return pl.pallas_call(
        final_kernel,
        out_shape=outs,
        in_specs=[pl.BlockSpec(memory_space=pl.ANY)] * len(args),
        out_specs=[vm] * len(outs),
        scratch_shapes=[VMEM(a.shape, a.dtype) for a in args[:3] + args[4:]]
        + [VMEM((32, 64), F32), VMEM((32, 768), F32), pltpu.SemaphoreType.DMA((8,))],
        compiler_params=pltpu.CompilerParams(vmem_limit_bytes=62 * 2**20),
        name="final_layout",
    )(*args)


def on_device(
    hidden,
    condition,
    caption,
    lengths,
    frames,
    widths,
    caption_lens,
    cotangent,
    ada_weight,
    ada_bias,
    norm_gains,
    qkv_weight,
    head_gains,
    caption_weight,
    head_gate,
    out_weight,
    ffn_weight,
    down_weight,
):
    (
        w_f,
        w_a,
        cap_flip,
        first_flip,
        q8,
        kk,
        vv,
        qr,
        kr,
        tkr,
        other,
        lse,
        cw,
        cos_t,
        sin_t,
        resid,
        tk,
        tv,
        attn,
        middle,
        second_in,
        cot,
        mod_rows,
        gains,
        got1,
        live,
        facts,
    ) = attention_call(
        [
            hidden[:, 0],
            cotangent[:, 0],
            caption[:, 0],
            condition[:, 0],
            norm_gains,
            ada_weight,
            qkv_weight,
            out_weight,
            ffn_weight,
            down_weight.T,
            jnp.transpose(caption_weight, (0, 2, 1)),
            ada_bias[None],
            head_gains,
            head_gate[None],
            lengths.T,
            frames.T,
            widths.T,
            caption_lens.T,
        ],
        1,
    )
    layer_out, grad_middle, grad_attn_in, dw_half, ffn_sums = ffn_call(
        second_in,
        w_f.reshape(2, D, D),
        middle,
        attn,
        cot.reshape(128, D),
        mod_rows,
        gains,
        live,
        2,
    )
    d_out, f_out, c_out, layer_final, hidden_final, g_all, gain_out = back_call(
        [
            dw_half,
            w_a,
            cap_flip,
            first_flip,
            q8,
            kk,
            vv,
            qr,
            kr,
            tkr,
            other,
            lse,
            cw,
            cos_t,
            sin_t,
            resid,
            tk,
            tv,
            grad_middle,
            grad_attn_in,
            layer_out.reshape(2, 64, D),
            mod_rows,
            gains,
            ffn_sums,
            facts,
        ],
        3,
    )
    (
        layer,
        grad_hidden,
        ada,
        bias,
        norm,
        qkv,
        heads,
        cap,
        gate,
        out_w,
        ffn,
        down,
    ) = final_call(
        [d_out, f_out, c_out, layer_final, hidden_final, g_all, gain_out, got1]
    )
    return (
        layer[:, None],
        grad_hidden[:, None],
        ada,
        bias[0],
        norm,
        qkv,
        heads,
        jnp.transpose(cap, (0, 2, 1)),
        gate[0],
        out_w,
        ffn,
        down.T,
    )


def solution(mesh):
    return jax.shard_map(
        on_device,
        mesh=mesh,
        in_specs=(
            P(None, "dp", "tensor", None),
            P(None, "dp", None),
            P(None, "dp", None, None),
            P(None, "dp"),
            P(None, "dp"),
            P(None, "dp"),
            P(None, "dp"),
            P(None, "dp", "tensor", None),
            P("dp", "tensor"),
            P("dp"),
            P(None, "dp"),
            P(None, "dp", "tensor"),
            P(),
            P(None, "dp", "tensor"),
            P(),
            P("tensor", "dp"),
            P(None, "dp", "tensor"),
            P("tensor", "dp"),
        ),
        out_specs=(
            P(None, "dp", "tensor", None),
            P(None, "dp", "tensor", None),
            P("dp", "tensor"),
            P("dp"),
            P(None, "dp"),
            P(None, "dp", "tensor"),
            P(),
            P(None, "dp", "tensor"),
            P(),
            P("tensor", "dp"),
            P(None, "dp", "tensor"),
            P("tensor", "dp"),
        ),
        check_vma=False,
    )
```

profile of v0, /device:TPU:1, one launch (start us, length us, event | category | flops | bytes accessed | tf_op | source)
XLA Modules:
  0.0 256.2 jit_solution(11610234097329404248)
XLA Ops:
  0.6 1.2 broadcast_in_dim.12.bias_ref
  1.9 90.5 %attention.1 = (bf16[2,2,4,2,96,1536]{5,4,3,2,1,0:T(8,128)(2,1)}, bf16[2,2,4,2,96,768]{5,4,3,2,1,0:T(8,128)(2,1)}, bf16[4096,256]{1,0:T(8,128)(2,1)}, bf16[1536,...) custom-call(bf16[2,64,1536]{2,1,0:T(8,128)(2,1)} %bitcast.26, ...), custom_call_target="tpu_custom_call" | custom-call | tf_op jit(solution)/shard_map/attention/pallas_call | solution.py:783
  92.4 74.2 %ffn.1 = (bf16[128,1536]{1,0:T(8,128)(2,1)}, f32[128,1536]{1,0:T(8,128)}, bf16[128,1536]{1,0:T(8,128)(2,1)}, bf16[2,2,4,96,1536]{4,3,2,1,0:T(8,128)(2,1)}, f32[8,1536]{1,0:T(8,128)}) custom-call(bf16[128,1536]{1,0:T(8,128)(2,1)} %get-tuple-element.63.x_ref, bf16[2,1536,1536]{2,1,0:T(8,128)(2,1)} %bitcast.23, f32[128,1536]{1,0:T(8,128)} %get-tuple-element.65.mid_in, ...), custom_call_target="tpu_custom_call" | custom-call | tf_op jit(solution)/shard_map/ffn/pallas_call | solution.py:1058
  166.7 84.8 %attention_back.1 = (f32[96,768]{1,0:T(8,128)}, f32[96,1536]{1,0:T(8,128)}, f32[256,384]{1,0:T(8,128)}, bf16[2,64,1536]{2,1,0:T(8,128)(2,1)}, bf16[2,64,1536]{2,...) custom-call(bf16[2,2,4,96,1536]{4,3,2,1,0:T(8,128)(2,1)} %get-tuple-element.71.sib_in, ...), custom_call_target="tpu_custom_call" | custom-call | tf_op jit(solution)/shard_map/attention_back/pallas_call | solution.py:1659
  251.5 3.4 %final_layout.1 = (bf16[2,64,1536]{2,1,0:T(8,128)(2,1)}, f32[2,64,1536]{2,1,0:T(8,128)}, f32[64,768]{1,0:T(8,128)}, f32[1,384]{1,0:T(1,128)}, f32[4,96]{1,0:T(4,...) custom-call(f32[96,768]{1,0:T(8,128)} %get-tuple-element.94.d_in, ...), custom_call_target="tpu_custom_call" | custom-call | tf_op jit(solution)/shard_map/final_layout/pallas_call | solution.py:1800
  254.9 1.3 reduce
where the time goes:
time: 256 us
  Pallas kernels  253 us (99%)
    pallas_call x1, Pallas kernels, attention_call(): pl.pallas_call(attention_kernel, out_shape=[S((2, 2, 4, 2, 96, D), BF16)]...  90.5 us
    pallas_call x1, Pallas kernels, back_call(): pl.pallas_call(back_kernel, out_shape=outs, in_specs=[any_] * 21 + [vm] *...  84.8 us
    pallas_call x1, Pallas kernels, ffn_call(): pl.pallas_call(ffn_kernel, out_shape=[S((128, D), BF16), S((128, D), F32)...  74.2 us

commit v1 on v0

--- a/solution.py
+++ b/solution.py
@@ -455,7 +455,7 @@
         gain = head_gain_ref[i : i + 1, :].astype(F32)
         facts[i : i + 1, 0:64] = gain
         facts[i : i + 1, 64:128] = gain
-        facts[BIAS_ROW + i : BIAS_ROW + i + 1, :] = bias_ref[:, i * 128 : i * 128 + 128].astype(F32)
+        facts[BIAS_ROW + i : BIAS_ROW + i + 1, :] = bias_ref[i * 128 : i * 128 + 128].astype(F32).reshape(1, 128)
     gates = jnp.tanh(head_gate_ref[...].astype(F32))
     gate_lane = lanes((1, 24))
     low_row = lanes((1, 128)) < 64
@@ -573,13 +573,13 @@
 
     lax.fori_loop(0, 3, scale_rows, 0)
     ga.step4()
+    gc.step3()
+    gf.start(local_sems.at[3])
     far_r.wait_recv()
     far_l.wait_recv()
     scale_rows(3, 0)
     resid_ref[...] = hid_all[0].reshape(128, D)
     flush(resid_ref, resid_out)
-    gc.step3()
-    gf.start(local_sems.at[3])
     transpose_into(first, first_flip)
     flush(first_flip, first_flip_out)
     lax.fori_loop(0, 32, flip_caption, 0)
@@ -1486,9 +1486,9 @@
     transpose_into(grad_all, flip)
     over_pairs(1, 2, (0,))
     scat_f.step3()
-    over_pairs(3, 1, (0,))
     scat_c.add()
     scat_c.first()
+    over_pairs(3, 1, (0,))
     cos = cos_ref[...].reshape(512, 128)
     sin = sin_ref[...].reshape(512, 128)
     low_head = lanes((512, 128)) < 64
@@ -1772,7 +1772,7 @@
     low = (items[...] - high.astype(F32)).astype(BF16)
     ada[...] = mm_rows(unit_rows, high) + mm_rows(unit_rows, low)
     for j in range(3):
-        bias[:, j * 128 : j * 128 + 128] = gain_in[8 + j : 9 + j, :]
+        bias[j * 128 : j * 128 + 128] = gain_in[8 + j : 9 + j, :].reshape(128)
     gains[...] = gain_in[0:4, 0:96]
     heads[0:1, :] = gain_in[4:5, 0:64]
     heads[1:2, :] = gain_in[4:5, 64:128]
@@ -1787,7 +1787,7 @@
         S((2, 64, D), BF16),
         S((2, 64, D), F32),
         S((64, 768), F32),
-        S((1, 384), F32),
+        S((384,), F32),
         S((4, 96), F32),
         S((3, 96, 192), F32),
         S((3, 64), F32),
@@ -1870,7 +1870,7 @@
             ffn_weight,
             down_weight.T,
             jnp.transpose(caption_weight, (0, 2, 1)),
-            ada_bias[None],
+            ada_bias,
             head_gains,
             head_gate[None],
             lengths.T,
@@ -1941,7 +1941,7 @@
         layer[:, None],
         grad_hidden[:, None],
         ada,
-        bias[0],
+        bias,
         norm,
         qkv,
         heads,

time: 256 us -> 254 us (level)
  no operation moved by 1% of the time
where the time goes in v1:
time: 254 us
  Pallas kernels  253 us (100%)
    pallas_call x1, Pallas kernels, attention_call(): pl.pallas_call(attention_kernel, out_shape=[S((2, 2, 4, 2, 96, D), BF16)]...  90.7 us
    pallas_call x1, Pallas kernels, back_call(): pl.pallas_call(back_kernel, out_shape=outs, in_specs=[any_] * 21 + [vm] *...  84.5 us
    pallas_call x1, Pallas kernels, ffn_call(): pl.pallas_call(ffn_kernel, out_shape=[S((128, D), BF16), S((128, D), F32)...  74.2 us

profile of v1, /device:TPU:1, one launch (start us, length us, event | category | flops | bytes accessed | tf_op | source)
XLA Modules:
  0.0 253.6 jit_solution(6838214983052434814)
XLA Ops:
  0.7 90.7 %attention.1 = (bf16[2,2,4,2,96,1536]{5,4,3,2,1,0:T(8,128)(2,1)}, bf16[2,2,4,2,96,768]{5,4,3,2,1,0:T(8,128)(2,1)}, bf16[4096,256]{1,0:T(8,128)(2,1)}, bf16[1536,...) custom-call(bf16[2,64,1536]{2,1,0:T(8,128)(2,1)} %bitcast.26, ...), custom_call_target="tpu_custom_call" | custom-call | tf_op jit(solution)/shard_map/attention/pallas_call | solution.py:783
  91.3 74.2 %ffn.1 = (bf16[128,1536]{1,0:T(8,128)(2,1)}, f32[128,1536]{1,0:T(8,128)}, bf16[128,1536]{1,0:T(8,128)(2,1)}, bf16[2,2,4,96,1536]{4,3,2,1,0:T(8,128)(2,1)}, f32[8,1536]{1,0:T(8,128)}) custom-call(bf16[128,1536]{1,0:T(8,128)(2,1)} %get-tuple-element.63.x_ref, bf16[2,1536,1536]{2,1,0:T(8,128)(2,1)} %bitcast.23, f32[128,1536]{1,0:T(8,128)} %get-tuple-element.65.mid_in, ...), custom_call_target="tpu_custom_call" | custom-call | tf_op jit(solution)/shard_map/ffn/pallas_call | solution.py:1058
  165.5 84.5 %attention_back.1 = (f32[96,768]{1,0:T(8,128)}, f32[96,1536]{1,0:T(8,128)}, f32[256,384]{1,0:T(8,128)}, bf16[2,64,1536]{2,1,0:T(8,128)(2,1)}, bf16[2,64,1536]{2,...) custom-call(bf16[2,2,4,96,1536]{4,3,2,1,0:T(8,128)(2,1)} %get-tuple-element.71.sib_in, ...), custom_call_target="tpu_custom_call" | custom-call | tf_op jit(solution)/shard_map/attention_back/pallas_call | solution.py:1659
  250.0 3.4 %final_layout.1 = (bf16[2,64,1536]{2,1,0:T(8,128)(2,1)}, f32[2,64,1536]{2,1,0:T(8,128)}, f32[64,768]{1,0:T(8,128)}, f32[384]{0:T(512)}, f32[4,96]{1,0:T(4,128)},...) custom-call(f32[96,768]{1,0:T(8,128)} %get-tuple-element.94.d_in, ...), custom_call_target="tpu_custom_call" | custom-call | tf_op jit(solution)/shard_map/final_layout/pallas_call | solution.py:1800
